TPU v7x, 32 devices: a whole 2x2x4 slice. The times are simulated.
32 devices in a mesh: tile: 32 (over z, y, x, core), real: 1.
Axes of the slice: x: 2, y: 2, z: 4, core: 2. Of those that a mesh axis runs over, the one named last changes fastest.
Arguments:
- voltage: float32 [32, 32768], P('real', 'tile'), may hold values from -4 to 4
- recovery: float32 [32, 32768], P('real', 'tile'), may hold values from -3 to 3
- increments: float32 [10, 32, 32768], P(None, 'real', 'tile'), may hold values from -6 to 6
- band_weight: bfloat16 [32768, 3072], P('tile'), may hold values from -0.125 to 0.125
- time_scale: float32 [32768], P('tile'), may hold values from 0.05 to 0.5
- tract_in: bfloat16 [4, 32768, 256], P(None, 'tile'), may hold values from -0.375 to 0.375
- tract_out: bfloat16 [4, 32768, 256], P(None, 'tile'), may hold values from -0.1875 to 0.1875
- matching_masks: int32 [4], replicated, may hold values from 1 to 31, as said below
- tract_on: int32 [32, 4], P('tile'), may hold values 0 or 1
Outputs:
- voltage_end: float32 [32, 32768], P('real', 'tile')
- recovery_end: float32 [32, 32768], P('real', 'tile')
Inputs may be any that keep to these rules, and one draw needn't show every extreme that they name: `matching_masks`: the 4 masks are distinct.
All inputs are finite; a program needn't handle non-finite values. No bound on the sum of `tract_on` on one device may be relied on, other than what follows from the above.
Results may differ from a plain program's by a relative error of at most 0.0013.
Values may be sent and summed in bfloat16 or wider, within the bound.
A program may use at most 64 MiB of HBM per device.

v0:
```python
import math

import jax
import jax.numpy as jnp
from jax import lax
from jax.sharding import PartitionSpec as P

TILE_V = 1024
HW = 1024


time_step = 0.1
noise_gain = 0.5
shift_a = 0.7
damp_b = 0.8
drive_level = 0.5
band_gain = 1.0
tract_gain = 0.5


def padded_2(cells, sides, width):
    for axis, dim in sides:
        count = lax.axis_size(axis)
        ends = count - 1
        head = lax.slice_in_dim(cells, 0, width, axis=dim)
        tail = lax.slice_in_dim(cells, cells.shape[dim] - width, cells.shape[dim], axis=dim)
        cells = jnp.concatenate(
            [
                lax.ppermute(tail, axis, [(i, (i + 1) % count) for i in range(ends)]),
                cells,
                lax.ppermute(head, axis, [((i + 1) % count, i) for i in range(ends)]),
            ],
            axis=dim,
        )
    return cells


def swapped(block, axis, apart):
    count = lax.axis_size(axis)
    route = []
    for low in range(count):
        high = low | 1 << apart
        if high != low and high < count:
            route += [(low, high), (high, low)]
    return lax.ppermute(block, axis, route)


def contract_last(left, right):
    return lax.dot_general(
        left, right, (((1,), (1,)), ((), ())), preferred_element_type=jnp.float32
    )


def per_device(
    voltage,
    recovery,
    increments,
    band_weight,
    time_scale,
    tract_in,
    tract_out,
    matching_masks,
    tract_on,
):
    window_width = TILE_V + 2 * HW
    row_index = jnp.arange(TILE_V, dtype=jnp.int32)[:, None]
    col_index = jnp.arange(window_width, dtype=jnp.int32)[None, :]
    inband = (col_index - row_index >= 0) & (col_index - row_index <= 2 * HW)
    banded = jnp.where(inband, band_weight, jnp.zeros((), jnp.bfloat16))
    low_part = banded[:, :HW]
    own_part = banded[:, HW : HW + TILE_V]
    high_part = banded[:, HW + TILE_V :]
    tile_count = lax.axis_size("tile")
    bit_count = tile_count.bit_length() - 1
    bit_sequence = list(range(bit_count))
    tract_gate = tract_on[0].astype(jnp.bfloat16)

    def advance(step_index, state_pair):
        voltage_now, recovery_now = state_pair
        rounded = voltage_now.astype(jnp.bfloat16)
        padded = padded_2(rounded, (("tile", 1),), HW)
        band_drive = contract_last(rounded, own_part)
        band_drive = band_drive + contract_last(padded[:, :HW], low_part)
        band_drive = band_drive + contract_last(padded[:, HW + TILE_V :], high_part)
        projected = jnp.einsum(
            "rv,mvk->mrk", rounded, tract_out, preferred_element_type=jnp.float32
        ).astype(jnp.bfloat16)
        for bit in bit_sequence:
            arrived = swapped(projected, "tile", bit)
            chosen = jnp.bitwise_and(jnp.right_shift(matching_masks, bit), 1) == 1
            projected = jnp.where(chosen[:, None, None], arrived, projected)
        received = projected * tract_gate[:, None, None]
        tract_drive = jnp.einsum(
            "mrk,mvk->rv", received, tract_in, preferred_element_type=jnp.float32
        )
        kick_now = lax.dynamic_index_in_dim(increments, step_index, 0, keepdims=False)
        total_drive = band_gain * band_drive + tract_gain * tract_drive + drive_level
        voltage_new = (
            voltage_now
            + time_step * (voltage_now - voltage_now**3 / 3.0 - recovery_now + total_drive)
            + noise_gain * math.sqrt(time_step) * kick_now
        )
        recovery_new = recovery_now + time_step * time_scale[None, :] * (
            voltage_now + shift_a - damp_b * recovery_now
        )
        return (voltage_new, recovery_new)

    voltage_end, recovery_end = lax.fori_loop(0, increments.shape[0], advance, (voltage, recovery))
    return (voltage_end, recovery_end)


def solution(mesh):
    placed = (
        P("real", "tile"),
        P("real", "tile"),
        P(None, "real", "tile"),
        P("tile", None),
        P("tile"),
        P(None, "tile", None),
        P(None, "tile", None),
        P(),
        P("tile", None),
    )
    return jax.shard_map(
        per_device,
        mesh=mesh,
        in_specs=placed,
        out_specs=(P("real", "tile"), P("real", "tile")),
        check_vma=False,
    )
```

profile of v0, /device:TPU:0, one launch (start us, length us, event | category | flops | bytes accessed | tf_op | source)
XLA Modules:
  0.0 296.1 jit_solution(3992501936836388201)
XLA Ops:
  0.6 3.5 %fusion.19 = bf16[1024,3072]{1,0:T(8,128)(2,1)S(1)} fusion(bf16[1024,3072]{1,0:T(8,128)(2,1)} %param.14), kind=kLoop, calls=%fused_computation.36 | loop fusion | flops 15728640 | bytes 12582912 | tf_op jit(solution)/shard_map/jit(_where)/select_n | solution.py:69
  6.9 288.5 %while.15 = (s32[]{:T(128)}, f32[32,1024]{1,0:T(8,128)S(1)}, f32[32,1024]{1,0:T(8,128)S(1)}, bf16[1024,1024]{1,0:T(8,128)(2,1)}, bf16[1024,1024]{1,0:T(8,128)(2,...) while((s32[]{:T(128)}, f32[32,1024]{1,0:T(8,128)S(1)}, ...), condition=%wide.region_1.2_spmd, body=%wide.region_0.1_spmd.sunk | while | flops 336462912 | bytes 32387608 | solution.py:108
  10.7 2.9 collective-permute-start.1
  20.6 6.4 %collective-permute-start.3 = (bf16[4,32,256]{2,1,0:T(8,128)(2,1)S(1)}, bf16[4,32,256]{2,1,0:T(8,128)(2,1)S(1)}, u32[]{:S(2)}, u32[]{:S(2)}) collective-permute-start(bf16[4,32,256]{2,1,0:T(8,128)(2,1)S(1)} %broadcast_select_fusion.10), channel_id=1, source_target_pairs={{0,8},{8,0},{1,9},{9,1},{2,10},{10,2},{3,11},{11,3},{4,12},{12,4},... | collective-permute-start | bytes 196616 | tf_op jit(solution)/shard_map/while/body/eval_jaxpr/ppermute | solution.py:45
  29.9 3.3 %collective-permute-start.4 = (bf16[4,32,256]{2,1,0:T(8,128)(2,1)S(1)}, bf16[4,32,256]{2,1,0:T(8,128)(2,1)S(1)}, u32[]{:S(2)}, u32[]{:S(2)}) collective-permute-start(bf16[4,32,256]{2,1,0:T(8,128)(2,1)S(1)} %broadcast_select_fusion.11), channel_id=1, source_target_pairs={{0,16},{16,0},{1,17},{17,1},{2,18},{18,2},{3,19},{19,3},{4,20},{20... | collective-permute-start | bytes 196616 | tf_op jit(solution)/shard_map/while/body/eval_jaxpr/ppermute | solution.py:45
  42.2 4.3 %collective-permute-done.1 = bf16[4,32,256]{2,1,0:T(8,128)(2,1)S(1)} collective-permute-done((bf16[4,32,256]{2,1,0:T(8,128)(2,1)S(1)}, bf16[4,32,256]{2,1,0:T(8,128)(2,1)S(1)}, u32[]{:S(2)}, u32[]{:S(2)}) %collective-permute-start.1) | collective-permute-done | bytes 65568 | tf_op jit(solution)/shard_map/while/body/eval_jaxpr/ppermute | solution.py:45
  50.9 3.7 %collective-permute-start.3 = (bf16[4,32,256]{2,1,0:T(8,128)(2,1)S(1)}, bf16[4,32,256]{2,1,0:T(8,128)(2,1)S(1)}, u32[]{:S(2)}, u32[]{:S(2)}) collective-permute-start(bf16[4,32,256]{2,1,0:T(8,128)(2,1)S(1)} %broadcast_select_fusion.10), channel_id=1, source_target_pairs={{0,8},{8,0},{1,9},{9,1},{2,10},{10,2},{3,11},{11,3},{4,12},{12,4},... | collective-permute-start | bytes 196616 | tf_op jit(solution)/shard_map/while/body/eval_jaxpr/ppermute | solution.py:45
  57.4 3.4 %collective-permute-start.4 = (bf16[4,32,256]{2,1,0:T(8,128)(2,1)S(1)}, bf16[4,32,256]{2,1,0:T(8,128)(2,1)S(1)}, u32[]{:S(2)}, u32[]{:S(2)}) collective-permute-start(bf16[4,32,256]{2,1,0:T(8,128)(2,1)S(1)} %broadcast_select_fusion.11), channel_id=1, source_target_pairs={{0,16},{16,0},{1,17},{17,1},{2,18},{18,2},{3,19},{19,3},{4,20},{20... | collective-permute-start | bytes 196616 | tf_op jit(solution)/shard_map/while/body/eval_jaxpr/ppermute | solution.py:45
  70.3 3.9 %collective-permute-done.1 = bf16[4,32,256]{2,1,0:T(8,128)(2,1)S(1)} collective-permute-done((bf16[4,32,256]{2,1,0:T(8,128)(2,1)S(1)}, bf16[4,32,256]{2,1,0:T(8,128)(2,1)S(1)}, u32[]{:S(2)}, u32[]{:S(2)}) %collective-permute-start.1) | collective-permute-done | bytes 65568 | tf_op jit(solution)/shard_map/while/body/eval_jaxpr/ppermute | solution.py:45
  78.6 4.6 %collective-permute-start.3 = (bf16[4,32,256]{2,1,0:T(8,128)(2,1)S(1)}, bf16[4,32,256]{2,1,0:T(8,128)(2,1)S(1)}, u32[]{:S(2)}, u32[]{:S(2)}) collective-permute-start(bf16[4,32,256]{2,1,0:T(8,128)(2,1)S(1)} %broadcast_select_fusion.10), channel_id=1, source_target_pairs={{0,8},{8,0},{1,9},{9,1},{2,10},{10,2},{3,11},{11,3},{4,12},{12,4},... | collective-permute-start | bytes 196616 | tf_op jit(solution)/shard_map/while/body/eval_jaxpr/ppermute | solution.py:45
  86.1 3.1 %collective-permute-start.4 = (bf16[4,32,256]{2,1,0:T(8,128)(2,1)S(1)}, bf16[4,32,256]{2,1,0:T(8,128)(2,1)S(1)}, u32[]{:S(2)}, u32[]{:S(2)}) collective-permute-start(bf16[4,32,256]{2,1,0:T(8,128)(2,1)S(1)} %broadcast_select_fusion.11), channel_id=1, source_target_pairs={{0,16},{16,0},{1,17},{17,1},{2,18},{18,2},{3,19},{19,3},{4,20},{20... | collective-permute-start | bytes 196616 | tf_op jit(solution)/shard_map/while/body/eval_jaxpr/ppermute | solution.py:45
  97.7 4.2 %collective-permute-done.1 = bf16[4,32,256]{2,1,0:T(8,128)(2,1)S(1)} collective-permute-done((bf16[4,32,256]{2,1,0:T(8,128)(2,1)S(1)}, bf16[4,32,256]{2,1,0:T(8,128)(2,1)S(1)}, u32[]{:S(2)}, u32[]{:S(2)}) %collective-permute-start.1) | collective-permute-done | bytes 65568 | tf_op jit(solution)/shard_map/while/body/eval_jaxpr/ppermute | solution.py:45
  106.4 4.8 %collective-permute-start.3 = (bf16[4,32,256]{2,1,0:T(8,128)(2,1)S(1)}, bf16[4,32,256]{2,1,0:T(8,128)(2,1)S(1)}, u32[]{:S(2)}, u32[]{:S(2)}) collective-permute-start(bf16[4,32,256]{2,1,0:T(8,128)(2,1)S(1)} %broadcast_select_fusion.10), channel_id=1, source_target_pairs={{0,8},{8,0},{1,9},{9,1},{2,10},{10,2},{3,11},{11,3},{4,12},{12,4},... | collective-permute-start | bytes 196616 | tf_op jit(solution)/shard_map/while/body/eval_jaxpr/ppermute | solution.py:45
  114.0 3.7 %collective-permute-start.4 = (bf16[4,32,256]{2,1,0:T(8,128)(2,1)S(1)}, bf16[4,32,256]{2,1,0:T(8,128)(2,1)S(1)}, u32[]{:S(2)}, u32[]{:S(2)}) collective-permute-start(bf16[4,32,256]{2,1,0:T(8,128)(2,1)S(1)} %broadcast_select_fusion.11), channel_id=1, source_target_pairs={{0,16},{16,0},{1,17},{17,1},{2,18},{18,2},{3,19},{19,3},{4,20},{20... | collective-permute-start | bytes 196616 | tf_op jit(solution)/shard_map/while/body/eval_jaxpr/ppermute | solution.py:45
  126.3 4.2 %collective-permute-done.1 = bf16[4,32,256]{2,1,0:T(8,128)(2,1)S(1)} collective-permute-done((bf16[4,32,256]{2,1,0:T(8,128)(2,1)S(1)}, bf16[4,32,256]{2,1,0:T(8,128)(2,1)S(1)}, u32[]{:S(2)}, u32[]{:S(2)}) %collective-permute-start.1) | collective-permute-done | bytes 65568 | tf_op jit(solution)/shard_map/while/body/eval_jaxpr/ppermute | solution.py:45
  134.9 5.3 %collective-permute-start.3 = (bf16[4,32,256]{2,1,0:T(8,128)(2,1)S(1)}, bf16[4,32,256]{2,1,0:T(8,128)(2,1)S(1)}, u32[]{:S(2)}, u32[]{:S(2)}) collective-permute-start(bf16[4,32,256]{2,1,0:T(8,128)(2,1)S(1)} %broadcast_select_fusion.10), channel_id=1, source_target_pairs={{0,8},{8,0},{1,9},{9,1},{2,10},{10,2},{3,11},{11,3},{4,12},{12,4},... | collective-permute-start | bytes 196616 | tf_op jit(solution)/shard_map/while/body/eval_jaxpr/ppermute | solution.py:45
  143.3 3.6 %collective-permute-start.4 = (bf16[4,32,256]{2,1,0:T(8,128)(2,1)S(1)}, bf16[4,32,256]{2,1,0:T(8,128)(2,1)S(1)}, u32[]{:S(2)}, u32[]{:S(2)}) collective-permute-start(bf16[4,32,256]{2,1,0:T(8,128)(2,1)S(1)} %broadcast_select_fusion.11), channel_id=1, source_target_pairs={{0,16},{16,0},{1,17},{17,1},{2,18},{18,2},{3,19},{19,3},{4,20},{20... | collective-permute-start | bytes 196616 | tf_op jit(solution)/shard_map/while/body/eval_jaxpr/ppermute | solution.py:45
  155.3 4.3 %collective-permute-done.1 = bf16[4,32,256]{2,1,0:T(8,128)(2,1)S(1)} collective-permute-done((bf16[4,32,256]{2,1,0:T(8,128)(2,1)S(1)}, bf16[4,32,256]{2,1,0:T(8,128)(2,1)S(1)}, u32[]{:S(2)}, u32[]{:S(2)}) %collective-permute-start.1) | collective-permute-done | bytes 65568 | tf_op jit(solution)/shard_map/while/body/eval_jaxpr/ppermute | solution.py:45
  164.0 5.0 %collective-permute-start.3 = (bf16[4,32,256]{2,1,0:T(8,128)(2,1)S(1)}, bf16[4,32,256]{2,1,0:T(8,128)(2,1)S(1)}, u32[]{:S(2)}, u32[]{:S(2)}) collective-permute-start(bf16[4,32,256]{2,1,0:T(8,128)(2,1)S(1)} %broadcast_select_fusion.10), channel_id=1, source_target_pairs={{0,8},{8,0},{1,9},{9,1},{2,10},{10,2},{3,11},{11,3},{4,12},{12,4},... | collective-permute-start | bytes 196616 | tf_op jit(solution)/shard_map/while/body/eval_jaxpr/ppermute | solution.py:45
  172.2 3.2 %collective-permute-start.4 = (bf16[4,32,256]{2,1,0:T(8,128)(2,1)S(1)}, bf16[4,32,256]{2,1,0:T(8,128)(2,1)S(1)}, u32[]{:S(2)}, u32[]{:S(2)}) collective-permute-start(bf16[4,32,256]{2,1,0:T(8,128)(2,1)S(1)} %broadcast_select_fusion.11), channel_id=1, source_target_pairs={{0,16},{16,0},{1,17},{17,1},{2,18},{18,2},{3,19},{19,3},{4,20},{20... | collective-permute-start | bytes 196616 | tf_op jit(solution)/shard_map/while/body/eval_jaxpr/ppermute | solution.py:45
  183.8 4.3 %collective-permute-done.1 = bf16[4,32,256]{2,1,0:T(8,128)(2,1)S(1)} collective-permute-done((bf16[4,32,256]{2,1,0:T(8,128)(2,1)S(1)}, bf16[4,32,256]{2,1,0:T(8,128)(2,1)S(1)}, u32[]{:S(2)}, u32[]{:S(2)}) %collective-permute-start.1) | collective-permute-done | bytes 65568 | tf_op jit(solution)/shard_map/while/body/eval_jaxpr/ppermute | solution.py:45
  192.5 5.3 %collective-permute-start.3 = (bf16[4,32,256]{2,1,0:T(8,128)(2,1)S(1)}, bf16[4,32,256]{2,1,0:T(8,128)(2,1)S(1)}, u32[]{:S(2)}, u32[]{:S(2)}) collective-permute-start(bf16[4,32,256]{2,1,0:T(8,128)(2,1)S(1)} %broadcast_select_fusion.10), channel_id=1, source_target_pairs={{0,8},{8,0},{1,9},{9,1},{2,10},{10,2},{3,11},{11,3},{4,12},{12,4},... | collective-permute-start | bytes 196616 | tf_op jit(solution)/shard_map/while/body/eval_jaxpr/ppermute | solution.py:45
  200.9 3.6 %collective-permute-start.4 = (bf16[4,32,256]{2,1,0:T(8,128)(2,1)S(1)}, bf16[4,32,256]{2,1,0:T(8,128)(2,1)S(1)}, u32[]{:S(2)}, u32[]{:S(2)}) collective-permute-start(bf16[4,32,256]{2,1,0:T(8,128)(2,1)S(1)} %broadcast_select_fusion.11), channel_id=1, source_target_pairs={{0,16},{16,0},{1,17},{17,1},{2,18},{18,2},{3,19},{19,3},{4,20},{20... | collective-permute-start | bytes 196616 | tf_op jit(solution)/shard_map/while/body/eval_jaxpr/ppermute | solution.py:45
  212.9 4.3 %collective-permute-done.1 = bf16[4,32,256]{2,1,0:T(8,128)(2,1)S(1)} collective-permute-done((bf16[4,32,256]{2,1,0:T(8,128)(2,1)S(1)}, bf16[4,32,256]{2,1,0:T(8,128)(2,1)S(1)}, u32[]{:S(2)}, u32[]{:S(2)}) %collective-permute-start.1) | collective-permute-done | bytes 65568 | tf_op jit(solution)/shard_map/while/body/eval_jaxpr/ppermute | solution.py:45
  221.6 5.0 %collective-permute-start.3 = (bf16[4,32,256]{2,1,0:T(8,128)(2,1)S(1)}, bf16[4,32,256]{2,1,0:T(8,128)(2,1)S(1)}, u32[]{:S(2)}, u32[]{:S(2)}) collective-permute-start(bf16[4,32,256]{2,1,0:T(8,128)(2,1)S(1)} %broadcast_select_fusion.10), channel_id=1, source_target_pairs={{0,8},{8,0},{1,9},{9,1},{2,10},{10,2},{3,11},{11,3},{4,12},{12,4},... | collective-permute-start | bytes 196616 | tf_op jit(solution)/shard_map/while/body/eval_jaxpr/ppermute | solution.py:45
  229.8 3.2 %collective-permute-start.4 = (bf16[4,32,256]{2,1,0:T(8,128)(2,1)S(1)}, bf16[4,32,256]{2,1,0:T(8,128)(2,1)S(1)}, u32[]{:S(2)}, u32[]{:S(2)}) collective-permute-start(bf16[4,32,256]{2,1,0:T(8,128)(2,1)S(1)} %broadcast_select_fusion.11), channel_id=1, source_target_pairs={{0,16},{16,0},{1,17},{17,1},{2,18},{18,2},{3,19},{19,3},{4,20},{20... | collective-permute-start | bytes 196616 | tf_op jit(solution)/shard_map/while/body/eval_jaxpr/ppermute | solution.py:45
  241.5 4.3 %collective-permute-done.1 = bf16[4,32,256]{2,1,0:T(8,128)(2,1)S(1)} collective-permute-done((bf16[4,32,256]{2,1,0:T(8,128)(2,1)S(1)}, bf16[4,32,256]{2,1,0:T(8,128)(2,1)S(1)}, u32[]{:S(2)}, u32[]{:S(2)}) %collective-permute-start.1) | collective-permute-done | bytes 65568 | tf_op jit(solution)/shard_map/while/body/eval_jaxpr/ppermute | solution.py:45
  250.2 5.3 %collective-permute-start.3 = (bf16[4,32,256]{2,1,0:T(8,128)(2,1)S(1)}, bf16[4,32,256]{2,1,0:T(8,128)(2,1)S(1)}, u32[]{:S(2)}, u32[]{:S(2)}) collective-permute-start(bf16[4,32,256]{2,1,0:T(8,128)(2,1)S(1)} %broadcast_select_fusion.10), channel_id=1, source_target_pairs={{0,8},{8,0},{1,9},{9,1},{2,10},{10,2},{3,11},{11,3},{4,12},{12,4},... | collective-permute-start | bytes 196616 | tf_op jit(solution)/shard_map/while/body/eval_jaxpr/ppermute | solution.py:45
  258.5 3.6 %collective-permute-start.4 = (bf16[4,32,256]{2,1,0:T(8,128)(2,1)S(1)}, bf16[4,32,256]{2,1,0:T(8,128)(2,1)S(1)}, u32[]{:S(2)}, u32[]{:S(2)}) collective-permute-start(bf16[4,32,256]{2,1,0:T(8,128)(2,1)S(1)} %broadcast_select_fusion.11), channel_id=1, source_target_pairs={{0,16},{16,0},{1,17},{17,1},{2,18},{18,2},{3,19},{19,3},{4,20},{20... | collective-permute-start | bytes 196616 | tf_op jit(solution)/shard_map/while/body/eval_jaxpr/ppermute | solution.py:45
  270.6 4.3 %collective-permute-done.1 = bf16[4,32,256]{2,1,0:T(8,128)(2,1)S(1)} collective-permute-done((bf16[4,32,256]{2,1,0:T(8,128)(2,1)S(1)}, bf16[4,32,256]{2,1,0:T(8,128)(2,1)S(1)}, u32[]{:S(2)}, u32[]{:S(2)}) %collective-permute-start.1) | collective-permute-done | bytes 65568 | tf_op jit(solution)/shard_map/while/body/eval_jaxpr/ppermute | solution.py:45
  279.2 5.0 %collective-permute-start.3 = (bf16[4,32,256]{2,1,0:T(8,128)(2,1)S(1)}, bf16[4,32,256]{2,1,0:T(8,128)(2,1)S(1)}, u32[]{:S(2)}, u32[]{:S(2)}) collective-permute-start(bf16[4,32,256]{2,1,0:T(8,128)(2,1)S(1)} %broadcast_select_fusion.10), channel_id=1, source_target_pairs={{0,8},{8,0},{1,9},{9,1},{2,10},{10,2},{3,11},{11,3},{4,12},{12,4},... | collective-permute-start | bytes 196616 | tf_op jit(solution)/shard_map/while/body/eval_jaxpr/ppermute | solution.py:45
  287.4 3.2 %collective-permute-start.4 = (bf16[4,32,256]{2,1,0:T(8,128)(2,1)S(1)}, bf16[4,32,256]{2,1,0:T(8,128)(2,1)S(1)}, u32[]{:S(2)}, u32[]{:S(2)}) collective-permute-start(bf16[4,32,256]{2,1,0:T(8,128)(2,1)S(1)} %broadcast_select_fusion.11), channel_id=1, source_target_pairs={{0,16},{16,0},{1,17},{17,1},{2,18},{18,2},{3,19},{19,3},{4,20},{20... | collective-permute-start | bytes 196616 | tf_op jit(solution)/shard_map/while/body/eval_jaxpr/ppermute | solution.py:45
  (296 shorter events, 165.6 us)
Async XLA Ops:
  17.9 15.2 %collective-permute-start.5 = (bf16[32,1024]{1,0:T(8,128)(2,1)S(1)}, bf16[32,1024]{1,0:T(8,128)(2,1)S(1)}, u32[]{:S(2)}, u32[]{:S(2)}) collective-permute-start(bf16[32,1024]{1,0:T(8,128)(2,1)S(1)} %get-tuple-element.318), channel_id=1, source_target_pairs={{0,1},{1,2},{2,3},{3,4},{4,5},{5,6},{6,7},{7,8},{8,9},{9,10},{10,1... | collective-permute-start | bytes 196616 | tf_op jit(solution)/shard_map/while/body/eval_jaxpr/ppermute | solution.py:29
  19.2 17.6 %collective-permute-start.6 = (bf16[32,1024]{1,0:T(8,128)(2,1)S(1)}, bf16[32,1024]{1,0:T(8,128)(2,1)S(1)}, u32[]{:S(2)}, u32[]{:S(2)}) collective-permute-start(bf16[32,1024]{1,0:T(8,128)(2,1)S(1)} %get-tuple-element.318), channel_id=1, source_target_pairs={{1,0},{2,1},{3,2},{4,3},{5,4},{6,5},{7,6},{8,7},{9,8},{10,9},{11,1... | collective-permute-start | bytes 196616 | tf_op jit(solution)/shard_map/while/body/eval_jaxpr/ppermute | solution.py:31
  20.6 9.2 %collective-permute-start.3 = (bf16[4,32,256]{2,1,0:T(8,128)(2,1)S(1)}, bf16[4,32,256]{2,1,0:T(8,128)(2,1)S(1)}, u32[]{:S(2)}, u32[]{:S(2)}) collective-permute-start(bf16[4,32,256]{2,1,0:T(8,128)(2,1)S(1)} %broadcast_select_fusion.10), channel_id=1, source_target_pairs={{0,8},{8,0},{1,9},{9,1},{2,10},{10,2},{3,11},{11,3},{4,12},{12,4},... | collective-permute-start | bytes 196616 | tf_op jit(solution)/shard_map/while/body/eval_jaxpr/ppermute | solution.py:45
  29.9 6.2 %collective-permute-start.4 = (bf16[4,32,256]{2,1,0:T(8,128)(2,1)S(1)}, bf16[4,32,256]{2,1,0:T(8,128)(2,1)S(1)}, u32[]{:S(2)}, u32[]{:S(2)}) collective-permute-start(bf16[4,32,256]{2,1,0:T(8,128)(2,1)S(1)} %broadcast_select_fusion.11), channel_id=1, source_target_pairs={{0,16},{16,0},{1,17},{17,1},{2,18},{18,2},{3,19},{19,3},{4,20},{20... | collective-permute-start | bytes 196616 | tf_op jit(solution)/shard_map/while/body/eval_jaxpr/ppermute | solution.py:45
  46.5 14.3 %collective-permute-start.5 = (bf16[32,1024]{1,0:T(8,128)(2,1)S(1)}, bf16[32,1024]{1,0:T(8,128)(2,1)S(1)}, u32[]{:S(2)}, u32[]{:S(2)}) collective-permute-start(bf16[32,1024]{1,0:T(8,128)(2,1)S(1)} %get-tuple-element.318), channel_id=1, source_target_pairs={{0,1},{1,2},{2,3},{3,4},{4,5},{5,6},{6,7},{7,8},{8,9},{9,10},{10,1... | collective-permute-start | bytes 196616 | tf_op jit(solution)/shard_map/while/body/eval_jaxpr/ppermute | solution.py:29
  47.8 16.7 %collective-permute-start.6 = (bf16[32,1024]{1,0:T(8,128)(2,1)S(1)}, bf16[32,1024]{1,0:T(8,128)(2,1)S(1)}, u32[]{:S(2)}, u32[]{:S(2)}) collective-permute-start(bf16[32,1024]{1,0:T(8,128)(2,1)S(1)} %get-tuple-element.318), channel_id=1, source_target_pairs={{1,0},{2,1},{3,2},{4,3},{5,4},{6,5},{7,6},{8,7},{9,8},{10,9},{11,1... | collective-permute-start | bytes 196616 | tf_op jit(solution)/shard_map/while/body/eval_jaxpr/ppermute | solution.py:31
  50.9 6.5 %collective-permute-start.3 = (bf16[4,32,256]{2,1,0:T(8,128)(2,1)S(1)}, bf16[4,32,256]{2,1,0:T(8,128)(2,1)S(1)}, u32[]{:S(2)}, u32[]{:S(2)}) collective-permute-start(bf16[4,32,256]{2,1,0:T(8,128)(2,1)S(1)} %broadcast_select_fusion.10), channel_id=1, source_target_pairs={{0,8},{8,0},{1,9},{9,1},{2,10},{10,2},{3,11},{11,3},{4,12},{12,4},... | collective-permute-start | bytes 196616 | tf_op jit(solution)/shard_map/while/body/eval_jaxpr/ppermute | solution.py:45
  57.4 6.3 %collective-permute-start.4 = (bf16[4,32,256]{2,1,0:T(8,128)(2,1)S(1)}, bf16[4,32,256]{2,1,0:T(8,128)(2,1)S(1)}, u32[]{:S(2)}, u32[]{:S(2)}) collective-permute-start(bf16[4,32,256]{2,1,0:T(8,128)(2,1)S(1)} %broadcast_select_fusion.11), channel_id=1, source_target_pairs={{0,16},{16,0},{1,17},{17,1},{2,18},{18,2},{3,19},{19,3},{4,20},{20... | collective-permute-start | bytes 196616 | tf_op jit(solution)/shard_map/while/body/eval_jaxpr/ppermute | solution.py:45
  75.8 13.4 %collective-permute-start.5 = (bf16[32,1024]{1,0:T(8,128)(2,1)S(1)}, bf16[32,1024]{1,0:T(8,128)(2,1)S(1)}, u32[]{:S(2)}, u32[]{:S(2)}) collective-permute-start(bf16[32,1024]{1,0:T(8,128)(2,1)S(1)} %get-tuple-element.318), channel_id=1, source_target_pairs={{0,1},{1,2},{2,3},{3,4},{4,5},{5,6},{6,7},{7,8},{8,9},{9,10},{10,1... | collective-permute-start | bytes 196616 | tf_op jit(solution)/shard_map/while/body/eval_jaxpr/ppermute | solution.py:29
  77.1 15.2 %collective-permute-start.6 = (bf16[32,1024]{1,0:T(8,128)(2,1)S(1)}, bf16[32,1024]{1,0:T(8,128)(2,1)S(1)}, u32[]{:S(2)}, u32[]{:S(2)}) collective-permute-start(bf16[32,1024]{1,0:T(8,128)(2,1)S(1)} %get-tuple-element.318), channel_id=1, source_target_pairs={{1,0},{2,1},{3,2},{4,3},{5,4},{6,5},{7,6},{8,7},{9,8},{10,9},{11,1... | collective-permute-start | bytes 196616 | tf_op jit(solution)/shard_map/while/body/eval_jaxpr/ppermute | solution.py:31
  78.6 7.4 %collective-permute-start.3 = (bf16[4,32,256]{2,1,0:T(8,128)(2,1)S(1)}, bf16[4,32,256]{2,1,0:T(8,128)(2,1)S(1)}, u32[]{:S(2)}, u32[]{:S(2)}) collective-permute-start(bf16[4,32,256]{2,1,0:T(8,128)(2,1)S(1)} %broadcast_select_fusion.10), channel_id=1, source_target_pairs={{0,8},{8,0},{1,9},{9,1},{2,10},{10,2},{3,11},{11,3},{4,12},{12,4},... | collective-permute-start | bytes 196616 | tf_op jit(solution)/shard_map/while/body/eval_jaxpr/ppermute | solution.py:45
  103.4 14.4 %collective-permute-start.5 = (bf16[32,1024]{1,0:T(8,128)(2,1)S(1)}, bf16[32,1024]{1,0:T(8,128)(2,1)S(1)}, u32[]{:S(2)}, u32[]{:S(2)}) collective-permute-start(bf16[32,1024]{1,0:T(8,128)(2,1)S(1)} %get-tuple-element.318), channel_id=1, source_target_pairs={{0,1},{1,2},{2,3},{3,4},{4,5},{5,6},{6,7},{7,8},{8,9},{9,10},{10,1... | collective-permute-start | bytes 196616 | tf_op jit(solution)/shard_map/while/body/eval_jaxpr/ppermute | solution.py:29
  104.7 16.2 %collective-permute-start.6 = (bf16[32,1024]{1,0:T(8,128)(2,1)S(1)}, bf16[32,1024]{1,0:T(8,128)(2,1)S(1)}, u32[]{:S(2)}, u32[]{:S(2)}) collective-permute-start(bf16[32,1024]{1,0:T(8,128)(2,1)S(1)} %get-tuple-element.318), channel_id=1, source_target_pairs={{1,0},{2,1},{3,2},{4,3},{5,4},{6,5},{7,6},{8,7},{9,8},{10,9},{11,1... | collective-permute-start | bytes 196616 | tf_op jit(solution)/shard_map/while/body/eval_jaxpr/ppermute | solution.py:31
  106.4 7.6 %collective-permute-start.3 = (bf16[4,32,256]{2,1,0:T(8,128)(2,1)S(1)}, bf16[4,32,256]{2,1,0:T(8,128)(2,1)S(1)}, u32[]{:S(2)}, u32[]{:S(2)}) collective-permute-start(bf16[4,32,256]{2,1,0:T(8,128)(2,1)S(1)} %broadcast_select_fusion.10), channel_id=1, source_target_pairs={{0,8},{8,0},{1,9},{9,1},{2,10},{10,2},{3,11},{11,3},{4,12},{12,4},... | collective-permute-start | bytes 196616 | tf_op jit(solution)/shard_map/while/body/eval_jaxpr/ppermute | solution.py:45
  131.1 15.7 %collective-permute-start.5 = (bf16[32,1024]{1,0:T(8,128)(2,1)S(1)}, bf16[32,1024]{1,0:T(8,128)(2,1)S(1)}, u32[]{:S(2)}, u32[]{:S(2)}) collective-permute-start(bf16[32,1024]{1,0:T(8,128)(2,1)S(1)} %get-tuple-element.318), channel_id=1, source_target_pairs={{0,1},{1,2},{2,3},{3,4},{4,5},{5,6},{6,7},{7,8},{8,9},{9,10},{10,1... | collective-permute-start | bytes 196616 | tf_op jit(solution)/shard_map/while/body/eval_jaxpr/ppermute | solution.py:29
  132.4 17.5 %collective-permute-start.6 = (bf16[32,1024]{1,0:T(8,128)(2,1)S(1)}, bf16[32,1024]{1,0:T(8,128)(2,1)S(1)}, u32[]{:S(2)}, u32[]{:S(2)}) collective-permute-start(bf16[32,1024]{1,0:T(8,128)(2,1)S(1)} %get-tuple-element.318), channel_id=1, source_target_pairs={{1,0},{2,1},{3,2},{4,3},{5,4},{6,5},{7,6},{8,7},{9,8},{10,9},{11,1... | collective-permute-start | bytes 196616 | tf_op jit(solution)/shard_map/while/body/eval_jaxpr/ppermute | solution.py:31
  134.9 8.3 %collective-permute-start.3 = (bf16[4,32,256]{2,1,0:T(8,128)(2,1)S(1)}, bf16[4,32,256]{2,1,0:T(8,128)(2,1)S(1)}, u32[]{:S(2)}, u32[]{:S(2)}) collective-permute-start(bf16[4,32,256]{2,1,0:T(8,128)(2,1)S(1)} %broadcast_select_fusion.10), channel_id=1, source_target_pairs={{0,8},{8,0},{1,9},{9,1},{2,10},{10,2},{3,11},{11,3},{4,12},{12,4},... | collective-permute-start | bytes 196616 | tf_op jit(solution)/shard_map/while/body/eval_jaxpr/ppermute | solution.py:45
  159.7 15.7 %collective-permute-start.5 = (bf16[32,1024]{1,0:T(8,128)(2,1)S(1)}, bf16[32,1024]{1,0:T(8,128)(2,1)S(1)}, u32[]{:S(2)}, u32[]{:S(2)}) collective-permute-start(bf16[32,1024]{1,0:T(8,128)(2,1)S(1)} %get-tuple-element.318), channel_id=1, source_target_pairs={{0,1},{1,2},{2,3},{3,4},{4,5},{5,6},{6,7},{7,8},{8,9},{9,10},{10,1... | collective-permute-start | bytes 196616 | tf_op jit(solution)/shard_map/while/body/eval_jaxpr/ppermute | solution.py:29
  161.0 17.5 %collective-permute-start.6 = (bf16[32,1024]{1,0:T(8,128)(2,1)S(1)}, bf16[32,1024]{1,0:T(8,128)(2,1)S(1)}, u32[]{:S(2)}, u32[]{:S(2)}) collective-permute-start(bf16[32,1024]{1,0:T(8,128)(2,1)S(1)} %get-tuple-element.318), channel_id=1, source_target_pairs={{1,0},{2,1},{3,2},{4,3},{5,4},{6,5},{7,6},{8,7},{9,8},{10,9},{11,1... | collective-permute-start | bytes 196616 | tf_op jit(solution)/shard_map/while/body/eval_jaxpr/ppermute | solution.py:31
  164.0 8.1 %collective-permute-start.3 = (bf16[4,32,256]{2,1,0:T(8,128)(2,1)S(1)}, bf16[4,32,256]{2,1,0:T(8,128)(2,1)S(1)}, u32[]{:S(2)}, u32[]{:S(2)}) collective-permute-start(bf16[4,32,256]{2,1,0:T(8,128)(2,1)S(1)} %broadcast_select_fusion.10), channel_id=1, source_target_pairs={{0,8},{8,0},{1,9},{9,1},{2,10},{10,2},{3,11},{11,3},{4,12},{12,4},... | collective-permute-start | bytes 196616 | tf_op jit(solution)/shard_map/while/body/eval_jaxpr/ppermute | solution.py:45
  188.8 15.7 %collective-permute-start.5 = (bf16[32,1024]{1,0:T(8,128)(2,1)S(1)}, bf16[32,1024]{1,0:T(8,128)(2,1)S(1)}, u32[]{:S(2)}, u32[]{:S(2)}) collective-permute-start(bf16[32,1024]{1,0:T(8,128)(2,1)S(1)} %get-tuple-element.318), channel_id=1, source_target_pairs={{0,1},{1,2},{2,3},{3,4},{4,5},{5,6},{6,7},{7,8},{8,9},{9,10},{10,1... | collective-permute-start | bytes 196616 | tf_op jit(solution)/shard_map/while/body/eval_jaxpr/ppermute | solution.py:29
  190.1 17.5 %collective-permute-start.6 = (bf16[32,1024]{1,0:T(8,128)(2,1)S(1)}, bf16[32,1024]{1,0:T(8,128)(2,1)S(1)}, u32[]{:S(2)}, u32[]{:S(2)}) collective-permute-start(bf16[32,1024]{1,0:T(8,128)(2,1)S(1)} %get-tuple-element.318), channel_id=1, source_target_pairs={{1,0},{2,1},{3,2},{4,3},{5,4},{6,5},{7,6},{8,7},{9,8},{10,9},{11,1... | collective-permute-start | bytes 196616 | tf_op jit(solution)/shard_map/while/body/eval_jaxpr/ppermute | solution.py:31
  192.5 8.3 %collective-permute-start.3 = (bf16[4,32,256]{2,1,0:T(8,128)(2,1)S(1)}, bf16[4,32,256]{2,1,0:T(8,128)(2,1)S(1)}, u32[]{:S(2)}, u32[]{:S(2)}) collective-permute-start(bf16[4,32,256]{2,1,0:T(8,128)(2,1)S(1)} %broadcast_select_fusion.10), channel_id=1, source_target_pairs={{0,8},{8,0},{1,9},{9,1},{2,10},{10,2},{3,11},{11,3},{4,12},{12,4},... | collective-permute-start | bytes 196616 | tf_op jit(solution)/shard_map/while/body/eval_jaxpr/ppermute | solution.py:45
  217.3 15.7 %collective-permute-start.5 = (bf16[32,1024]{1,0:T(8,128)(2,1)S(1)}, bf16[32,1024]{1,0:T(8,128)(2,1)S(1)}, u32[]{:S(2)}, u32[]{:S(2)}) collective-permute-start(bf16[32,1024]{1,0:T(8,128)(2,1)S(1)} %get-tuple-element.318), channel_id=1, source_target_pairs={{0,1},{1,2},{2,3},{3,4},{4,5},{5,6},{6,7},{7,8},{8,9},{9,10},{10,1... | collective-permute-start | bytes 196616 | tf_op jit(solution)/shard_map/while/body/eval_jaxpr/ppermute | solution.py:29
  218.6 17.5 %collective-permute-start.6 = (bf16[32,1024]{1,0:T(8,128)(2,1)S(1)}, bf16[32,1024]{1,0:T(8,128)(2,1)S(1)}, u32[]{:S(2)}, u32[]{:S(2)}) collective-permute-start(bf16[32,1024]{1,0:T(8,128)(2,1)S(1)} %get-tuple-element.318), channel_id=1, source_target_pairs={{1,0},{2,1},{3,2},{4,3},{5,4},{6,5},{7,6},{8,7},{9,8},{10,9},{11,1... | collective-permute-start | bytes 196616 | tf_op jit(solution)/shard_map/while/body/eval_jaxpr/ppermute | solution.py:31
  221.6 8.1 %collective-permute-start.3 = (bf16[4,32,256]{2,1,0:T(8,128)(2,1)S(1)}, bf16[4,32,256]{2,1,0:T(8,128)(2,1)S(1)}, u32[]{:S(2)}, u32[]{:S(2)}) collective-permute-start(bf16[4,32,256]{2,1,0:T(8,128)(2,1)S(1)} %broadcast_select_fusion.10), channel_id=1, source_target_pairs={{0,8},{8,0},{1,9},{9,1},{2,10},{10,2},{3,11},{11,3},{4,12},{12,4},... | collective-permute-start | bytes 196616 | tf_op jit(solution)/shard_map/while/body/eval_jaxpr/ppermute | solution.py:45
  246.4 15.7 %collective-permute-start.5 = (bf16[32,1024]{1,0:T(8,128)(2,1)S(1)}, bf16[32,1024]{1,0:T(8,128)(2,1)S(1)}, u32[]{:S(2)}, u32[]{:S(2)}) collective-permute-start(bf16[32,1024]{1,0:T(8,128)(2,1)S(1)} %get-tuple-element.318), channel_id=1, source_target_pairs={{0,1},{1,2},{2,3},{3,4},{4,5},{5,6},{6,7},{7,8},{8,9},{9,10},{10,1... | collective-permute-start | bytes 196616 | tf_op jit(solution)/shard_map/while/body/eval_jaxpr/ppermute | solution.py:29
  247.7 17.5 %collective-permute-start.6 = (bf16[32,1024]{1,0:T(8,128)(2,1)S(1)}, bf16[32,1024]{1,0:T(8,128)(2,1)S(1)}, u32[]{:S(2)}, u32[]{:S(2)}) collective-permute-start(bf16[32,1024]{1,0:T(8,128)(2,1)S(1)} %get-tuple-element.318), channel_id=1, source_target_pairs={{1,0},{2,1},{3,2},{4,3},{5,4},{6,5},{7,6},{8,7},{9,8},{10,9},{11,1... | collective-permute-start | bytes 196616 | tf_op jit(solution)/shard_map/while/body/eval_jaxpr/ppermute | solution.py:31
  250.2 8.3 %collective-permute-start.3 = (bf16[4,32,256]{2,1,0:T(8,128)(2,1)S(1)}, bf16[4,32,256]{2,1,0:T(8,128)(2,1)S(1)}, u32[]{:S(2)}, u32[]{:S(2)}) collective-permute-start(bf16[4,32,256]{2,1,0:T(8,128)(2,1)S(1)} %broadcast_select_fusion.10), channel_id=1, source_target_pairs={{0,8},{8,0},{1,9},{9,1},{2,10},{10,2},{3,11},{11,3},{4,12},{12,4},... | collective-permute-start | bytes 196616 | tf_op jit(solution)/shard_map/while/body/eval_jaxpr/ppermute | solution.py:45
  274.9 15.7 %collective-permute-start.5 = (bf16[32,1024]{1,0:T(8,128)(2,1)S(1)}, bf16[32,1024]{1,0:T(8,128)(2,1)S(1)}, u32[]{:S(2)}, u32[]{:S(2)}) collective-permute-start(bf16[32,1024]{1,0:T(8,128)(2,1)S(1)} %get-tuple-element.318), channel_id=1, source_target_pairs={{0,1},{1,2},{2,3},{3,4},{4,5},{5,6},{6,7},{7,8},{8,9},{9,10},{10,1... | collective-permute-start | bytes 196616 | tf_op jit(solution)/shard_map/while/body/eval_jaxpr/ppermute | solution.py:29
  276.2 17.5 %collective-permute-start.6 = (bf16[32,1024]{1,0:T(8,128)(2,1)S(1)}, bf16[32,1024]{1,0:T(8,128)(2,1)S(1)}, u32[]{:S(2)}, u32[]{:S(2)}) collective-permute-start(bf16[32,1024]{1,0:T(8,128)(2,1)S(1)} %get-tuple-element.318), channel_id=1, source_target_pairs={{1,0},{2,1},{3,2},{4,3},{5,4},{6,5},{7,6},{8,7},{9,8},{10,9},{11,1... | collective-permute-start | bytes 196616 | tf_op jit(solution)/shard_map/while/body/eval_jaxpr/ppermute | solution.py:31
  279.2 8.1 %collective-permute-start.3 = (bf16[4,32,256]{2,1,0:T(8,128)(2,1)S(1)}, bf16[4,32,256]{2,1,0:T(8,128)(2,1)S(1)}, u32[]{:S(2)}, u32[]{:S(2)}) collective-permute-start(bf16[4,32,256]{2,1,0:T(8,128)(2,1)S(1)} %broadcast_select_fusion.10), channel_id=1, source_target_pairs={{0,8},{8,0},{1,9},{9,1},{2,10},{10,2},{3,11},{11,3},{4,12},{12,4},... | collective-permute-start | bytes 196616 | tf_op jit(solution)/shard_map/while/body/eval_jaxpr/ppermute | solution.py:45
  (65 other events, 417.7 us)
where the time goes:
time: 297 us; the launch traced here: 296 us
  starting transfers between devices  121 us (41%)
  waiting for transfers between devices  86.1 us (29%)
  matrix products  75.8 us (26%)
  other arithmetic  7.1 us (2%)
  local copies, waits for them, and re-layouts  3.58 us (1%)
    ppermute x50, starting transfers between devices, swapped(): return lax.ppermute(block, axis, route)  95.7 us
    ppermute x50, waiting for transfers between devices, swapped(): return lax.ppermute(block, axis, route)  85.9 us
    dot_general x30, matrix products, contract_last(): lax.dot_general(left, right, (((1,), (1,)), ((), ())), preferred_element_...  46.9 us
    dot_general x10, matrix products, advance(): jnp.einsum('rv,mvk->mrk', rounded, tract_out, preferred_element_type=jnp....  21.9 us
    ppermute x10, starting transfers between devices, padded_2(): lax.ppermute(head, axis, [((i + 1) % count, i) for i in range(ends)])  12.9 us
    ppermute x10, starting transfers between devices, padded_2(): lax.ppermute(tail, axis, [(i, (i + 1) % count) for i in range(ends)])  12.8 us
    dot_general x10, matrix products, advance(): jnp.einsum('mrk,mvk->rv', received, tract_in, preferred_element_type=jnp....  7.05 us
  transfers between devices with their start and end apart: 70, of which 41 were waited for; matrix products, arithmetic and copies ran while one was open for 13% of the time, Pallas kernels for 0%

commit v1 on v0

v1 whole, which is shorter than its diff:
```python
import functools
import math

import jax
import jax.numpy as jnp
from jax import lax
from jax.experimental import pallas as pl
from jax.experimental.pallas import tpu as pltpu
from jax.sharding import PartitionSpec as P

time_step = 0.1
noise_gain = 0.5
shift_a = 0.7
damp_b = 0.8
drive_level = 0.5
band_gain = 1.0
tract_gain = 0.5

MESH = pl.DeviceIdType.MESH
ROW_BLOCK = 256


def contract_last(left, right):
    return lax.dot_general(
        left, right, (((1,), (1,)), ((), ())), preferred_element_type=jnp.float32
    )


def field_kernel(
    tile_count,
    masks_ref,
    gate_ref,
    v_in,
    w_in,
    scale_in,
    kick_hbm,
    band_hbm,
    tin_hbm,
    tout_hbm,
    v_ref,
    w_ref,
    band,
    tin,
    tout,
    kicks,
    vb,
    left,
    right,
    acc,
    snd,
    rbuf,
    load_sem,
    halo_send,
    halo_recv,
    blk_send,
    blk_recv,
):
    steps = kicks.shape[0]
    match = tin.shape[0]
    rows, cols = v_in.shape
    hw = left.shape[2]
    blocks = cols // ROW_BLOCK
    span = band.shape[2]
    bits = tile_count.bit_length() - 1
    me = lax.axis_index("tile")

    def partner(bit):
        unit = 1 << bit
        return me + unit - 2 * unit * (lax.rem(me // unit, 2))

    loads_out = [
        pltpu.make_async_copy(tout_hbm.at[m], tout.at[m], load_sem.at[m]) for m in range(match)
    ]
    loads_band = [
        pltpu.make_async_copy(
            band_hbm.at[pl.ds(n * ROW_BLOCK, ROW_BLOCK), pl.ds(n * ROW_BLOCK, span)],
            band.at[n],
            load_sem.at[match + n],
        )
        for n in range(blocks)
    ]
    load_in = pltpu.make_async_copy(tin_hbm, tin, load_sem.at[match + blocks])
    load_kick = pltpu.make_async_copy(kick_hbm, kicks, load_sem.at[match + blocks + 1])
    for copy in loads_out + loads_band + [load_in, load_kick]:
        copy.start()

    has_left = me > 0
    has_right = me < tile_count - 1

    barrier = pltpu.get_barrier_semaphore()
    for bit in range(bits):
        pl.semaphore_signal(barrier, inc=1, device_id={"tile": partner(bit)}, device_id_type=MESH)

    @pl.when(has_left)
    def _():
        pl.semaphore_signal(barrier, inc=1, device_id={"tile": me - 1}, device_id_type=MESH)

    @pl.when(has_right)
    def _():
        pl.semaphore_signal(barrier, inc=1, device_id={"tile": me + 1}, device_id_type=MESH)

    v_ref[...] = v_in[...]
    w_ref[...] = w_in[...]

    @pl.when(me == 0)
    def _():
        left[...] = jnp.zeros_like(left)

    @pl.when(me == tile_count - 1)
    def _():
        right[...] = jnp.zeros_like(right)

    for copy in loads_out + loads_band + [load_in, load_kick]:
        copy.wait()
    row = lax.broadcasted_iota(jnp.int32, (ROW_BLOCK, ROW_BLOCK), 0)
    col = lax.broadcasted_iota(jnp.int32, (ROW_BLOCK, ROW_BLOCK), 1)
    for n in range(blocks):
        head = band[n, :, :ROW_BLOCK].astype(jnp.float32)
        band[n, :, :ROW_BLOCK] = jnp.where(col >= row, head, 0.0).astype(jnp.bfloat16)
        tail = band[n, :, span - ROW_BLOCK :].astype(jnp.float32)
        band[n, :, span - ROW_BLOCK :] = jnp.where(col <= row, tail, 0.0).astype(jnp.bfloat16)

    neighbours = bits + jnp.where(has_left, 1, 0) + jnp.where(has_right, 1, 0)
    pl.semaphore_wait(barrier, neighbours)

    def send_left(slot):
        return pltpu.make_async_remote_copy(
            src_ref=vb,
            dst_ref=right.at[slot],
            send_sem=halo_send.at[0],
            recv_sem=halo_recv.at[1, slot],
            device_id={"tile": me - 1},
            device_id_type=MESH,
        )

    def send_right(slot):
        return pltpu.make_async_remote_copy(
            src_ref=vb,
            dst_ref=left.at[slot],
            send_sem=halo_send.at[1],
            recv_sem=halo_recv.at[0, slot],
            device_id={"tile": me + 1},
            device_id_type=MESH,
        )

    def block_copy(slot, turn, m):
        return pltpu.make_async_remote_copy(
            src_ref=snd.at[turn, m],
            dst_ref=rbuf.at[slot, turn, m],
            send_sem=blk_send.at[turn, m],
            recv_sem=blk_recv.at[slot, turn, m],
            device_id={"tile": partner((turn + m) % bits)},
            device_id_type=MESH,
        )

    def own_band(n):
        start = hw - n * ROW_BLOCK
        acc[:, n * ROW_BLOCK : (n + 1) * ROW_BLOCK] = contract_last(
            vb[...], band[n, :, start : start + cols]
        )

    def halo_band(n, slot):
        low = hw - n * ROW_BLOCK
        high = (n + 1) * ROW_BLOCK
        where = slice(n * ROW_BLOCK, (n + 1) * ROW_BLOCK)
        acc[:, where] = (
            acc[:, where]
            + contract_last(left[slot, :, n * ROW_BLOCK :], band[n, :, :low])
            + contract_last(right[slot, :, :high], band[n, :, span - high :])
        )

    def step(at, carry):
        slot = lax.rem(at, 2)
        vb[...] = v_ref[...].astype(jnp.bfloat16)

        @pl.when(has_left)
        def _():
            send_left(slot).start()

        @pl.when(has_right)
        def _():
            send_right(slot).start()

        for m in range(match):
            snd[0, m] = jnp.dot(
                vb[...], tout[m], preferred_element_type=jnp.float32
            ).astype(jnp.bfloat16)
            block_copy(slot, 0, m).start()
        arrived = [None] * match
        for turn in range(bits):
            if turn == 0:
                for n in range(blocks):
                    own_band(n)
            if turn == 1:

                @pl.when(has_left)
                def _():
                    send_right(slot).wait_recv()

                @pl.when(has_right)
                def _():
                    send_left(slot).wait_recv()

                for n in range(blocks):
                    halo_band(n, slot)
            for m in range(match):
                block_copy(slot, turn, m).wait_recv()
                bit = (turn + m) % bits
                chosen = ((masks_ref[m] // (1 << bit)) % 2) == 1
                kept = jnp.where(chosen, rbuf[slot, turn, m], snd[turn, m])
                if turn < bits - 1:
                    snd[turn + 1, m] = kept
                    block_copy(slot, turn + 1, m).start()
                else:
                    arrived[m] = kept * gate_ref[0, m].astype(jnp.float32).astype(jnp.bfloat16)
        tract = contract_last(arrived[0], tin[0])
        for m in range(1, match):
            tract = tract + contract_last(arrived[m], tin[m])
        v = v_ref[...]
        w = w_ref[...]
        total = band_gain * acc[...] + tract_gain * tract + drive_level
        v_ref[...] = (
            v
            + time_step * (v - v * v * v / 3.0 - w + total)
            + noise_gain * math.sqrt(time_step) * kicks[at]
        )
        w_ref[...] = w + time_step * scale_in[...] * (v + shift_a - damp_b * w)

        @pl.when(has_left)
        def _():
            send_left(slot).wait_send()

        @pl.when(has_right)
        def _():
            send_right(slot).wait_send()

        for turn in range(bits):
            for m in range(match):
                block_copy(slot, turn, m).wait_send()
        return carry

    lax.fori_loop(0, steps, step, 0)


def per_device(
    voltage,
    recovery,
    increments,
    band_weight,
    time_scale,
    tract_in,
    tract_out,
    matching_masks,
    tract_on,
):
    tile_count = lax.axis_size("tile")
    bits = tile_count.bit_length() - 1
    rows, cols = voltage.shape
    steps = increments.shape[0]
    match, _, rank = tract_in.shape
    hw = (band_weight.shape[1] - cols) // 2
    blocks = cols // ROW_BLOCK
    span = 2 * hw + ROW_BLOCK
    vmem = pl.BlockSpec(memory_space=pltpu.VMEM)
    smem = pl.BlockSpec(memory_space=pltpu.SMEM)
    hbm = pl.BlockSpec(memory_space=pl.ANY)
    shape = jax.ShapeDtypeStruct((rows, cols), jnp.float32)
    return pl.pallas_call(
        functools.partial(field_kernel, tile_count),
        out_shape=(shape, shape),
        in_specs=[smem, smem, vmem, vmem, vmem, hbm, hbm, hbm, hbm],
        out_specs=(vmem, vmem),
        scratch_shapes=[
            pltpu.VMEM((blocks, ROW_BLOCK, span), jnp.bfloat16),
            pltpu.VMEM((match, cols, rank), jnp.bfloat16),
            pltpu.VMEM((match, cols, rank), jnp.bfloat16),
            pltpu.VMEM((steps, rows, cols), jnp.float32),
            pltpu.VMEM((rows, cols), jnp.bfloat16),
            pltpu.VMEM((2, rows, hw), jnp.bfloat16),
            pltpu.VMEM((2, rows, hw), jnp.bfloat16),
            pltpu.VMEM((rows, cols), jnp.float32),
            pltpu.VMEM((bits, match, rows, rank), jnp.bfloat16),
            pltpu.VMEM((2, bits, match, rows, rank), jnp.bfloat16),
            pltpu.SemaphoreType.DMA((match + blocks + 2,)),
            pltpu.SemaphoreType.DMA((2,)),
            pltpu.SemaphoreType.DMA((2, 2)),
            pltpu.SemaphoreType.DMA((bits, match)),
            pltpu.SemaphoreType.DMA((2, bits, match)),
        ],
        compiler_params=pltpu.CompilerParams(
            collective_id=0, has_side_effects=True, vmem_limit_bytes=50 * 1024 * 1024
        ),
    )(
        matching_masks,
        tract_on,
        voltage,
        recovery,
        time_scale[None, :],
        increments,
        band_weight,
        tract_in,
        tract_out,
    )


def solution(mesh):
    placed = (
        P("real", "tile"),
        P("real", "tile"),
        P(None, "real", "tile"),
        P("tile", None),
        P("tile"),
        P(None, "tile", None),
        P(None, "tile", None),
        P(),
        P("tile", None),
    )
    return jax.shard_map(
        per_device,
        mesh=mesh,
        in_specs=placed,
        out_specs=(P("real", "tile"), P("real", "tile")),
        check_vma=False,
    )
```

time: 297 us -> 179 us (0.60)
  Pallas kernels: 0 us -> 170 us
  starting transfers between devices: 121 us -> 0 us
  waiting for transfers between devices: 86.1 us -> 0 us
  matrix products: 75.8 us -> 0 us
  other arithmetic: 7.1 us -> 0 us
  local copies, waits for them, and re-layouts: 3.58 us -> 8.02 us
    pallas_call x0 -> x1, Pallas kernels: none -> 170 us  [per_device(): pl.pallas_call(functools.partial(field_kernel, tile_count), out_shape=(sh...]
    ppermute x70 -> x0, starting transfers between devices: 121 us -> none  [the longest x50 95.7 us: swapped(): return lax.ppermute(block, axis, route)]
    ppermute x70 -> x0, waiting for transfers between devices: 86.1 us -> none  [the longest x50 85.9 us: swapped(): return lax.ppermute(block, axis, route)]
    dot_general x50 -> x0, matrix products: 75.8 us -> none  [the longest x30 46.9 us: contract_last(): lax.dot_general(left, right, (((1,), (1,)), ((), ())), preferred_element_...]
    unnamed x14 -> x16, local copies, waits for them, and re-layouts: 0.72 us -> 8.02 us
    select_n x41 -> x0, other arithmetic: 6.66 us -> none  [the longest x1 3.51 us: per_device(): banded = jnp.where(inband, band_weight, jnp.zeros((), jnp.bfloat16))]
  transfers between devices with their start and end apart: 70 -> 0, of which waited for: 41 -> 0; matrix products, arithmetic and copies ran while one was open for 13% -> 0% of each run, Pallas kernels for 0% -> 0%
where the time goes in v1:
time: 179 us
  Pallas kernels  170 us (95%)
  local copies, waits for them, and re-layouts  8.02 us (4%)
    pallas_call x1, Pallas kernels, per_device(): pl.pallas_call(functools.partial(field_kernel, tile_count), out_shape=(sh...  170 us
    unnamed x16, local copies, waits for them, and re-layouts  8.02 us

profile of v1, /device:TPU:0, one launch (start us, length us, event | category | flops | bytes accessed | tf_op | source)
XLA Modules:
  0.0 178.7 jit_solution(7053866107016539634)
XLA Ops:
  0.6 0.0 copy-start
  0.6 1.6 copy-done
  2.2 0.0 copy-start.1
  2.2 1.3 copy-done.1
  3.5 0.0 copy-start.2
  3.5 0.9 copy-done.2
  4.4 0.0 copy-start.3
  4.4 0.9 copy-done.3
  5.4 0.0 copy-start.4
  5.4 0.7 copy-done.4
  6.0 0.0 copy-start.5
  6.0 0.7 copy-done.5
  6.7 0.0 copy-start.6
  6.7 0.7 copy-done.6
  7.4 170.1 %shard_map.104 = (f32[32,1024]{1,0:T(8,128)S(1)}, f32[32,1024]{1,0:T(8,128)S(1)}) custom-call(s32[4]{0:T(128)S(1)} %copy-done.5, s32[1,4]{1,0:T(1,128)S(1)} %copy-done.6, f32[32,1024]{1,0:T(8,128)S(1)} %copy-done.2, f32[32,1024]{1,0:T(8,128)S(1)} %copy-done.3, f32[1,1024]{1,0:T(1,128)S(1)} %bitcast.1, f32[10,32,1024]{2,1,0:T(8,128)S(1)} %copy-done.1, ...), custom_call_target="tpu_custom_call" | custom-call | tf_op jit(solution)/shard_map/pallas_call | solution.py:268
  177.4 0.7 copy.13
  178.1 0.7 copy.14
Async XLA Ops:
  0.6 1.6 copy-start
  2.2 1.3 copy-start.1
  3.5 0.9 copy-start.2
  4.4 0.9 copy-start.3
  5.4 0.7 copy-start.4
  6.0 0.7 copy-start.5
  6.7 0.7 copy-start.6

commit v2 on v1

--- a/solution.py
+++ b/solution.py
@@ -28,6 +28,7 @@
 
 def field_kernel(
     tile_count,
+    cap,
     masks_ref,
     gate_ref,
     v_in,
@@ -47,6 +48,7 @@
     left,
     right,
     acc,
+    blk,
     snd,
     rbuf,
     load_sem,
@@ -64,9 +66,56 @@
     bits = tile_count.bit_length() - 1
     me = lax.axis_index("tile")
 
-    def partner(bit):
-        unit = 1 << bit
-        return me + unit - 2 * unit * (lax.rem(me // unit, 2))
+    low_bits = bits // 2 + bits % 2
+    low_count = 1 << low_bits
+    high_count = 1 << (bits - low_bits)
+    offsets = list(range(1, low_count)) + [h << low_bits for h in range(1, high_count)]
+    slots = len(offsets) * cap
+
+    def partner(offset):
+        there = me
+        for bit in range(bits):
+            if (offset >> bit) & 1:
+                unit = 1 << bit
+                there = there + unit - 2 * unit * lax.rem(me // unit, 2)
+        return there
+
+    def as_int(flag):
+        return jnp.where(flag, 1, 0)
+
+    masks = [masks_ref[m] for m in range(match)]
+    lows = [mask % low_count for mask in masks]
+    highs = [mask // low_count for mask in masks]
+    clash = {}
+    for m in range(match):
+        for n in range(m):
+            clash[n, m] = as_int((lows[m] == lows[n]) & (lows[m] != 0)) + as_int(
+                (highs[m] == highs[n]) & (highs[m] != 0)
+            )
+    best = None
+    for pattern in range(1 << (match - 1)):
+        cost = 0
+        for (n, m), value in clash.items():
+            if ((pattern >> n) & 1) == ((pattern >> m) & 1):
+                cost = cost + value
+        key = cost * (1 << match) + pattern
+        best = key if best is None else jnp.minimum(best, key)
+    turns = [(best // (1 << m)) % 2 for m in range(match)]
+    route = []
+    for rnd in range(2):
+        keys = []
+        for m in range(match):
+            low_key = jnp.where(lows[m] == 0, -1, lows[m] - 1)
+            high_key = jnp.where(highs[m] == 0, -1, highs[m] + low_count - 2)
+            keys.append(jnp.where(turns[m] == rnd, low_key, high_key))
+        places = []
+        for m in range(match):
+            earlier = 0
+            for n in range(m):
+                earlier = earlier + as_int(keys[n] == keys[m])
+            places.append(jnp.where(keys[m] < 0, -1, keys[m] * cap + earlier))
+        route.append(places)
+    gates = [gate_ref[0, m] != 0 for m in range(match)]
 
     loads_out = [
         pltpu.make_async_copy(tout_hbm.at[m], tout.at[m], load_sem.at[m]) for m in range(match)
@@ -88,8 +137,10 @@
     has_right = me < tile_count - 1
 
     barrier = pltpu.get_barrier_semaphore()
-    for bit in range(bits):
-        pl.semaphore_signal(barrier, inc=1, device_id={"tile": partner(bit)}, device_id_type=MESH)
+    for offset in offsets:
+        pl.semaphore_signal(
+            barrier, inc=1, device_id={"tile": partner(offset)}, device_id_type=MESH
+        )
 
     @pl.when(has_left)
     def _():
@@ -110,17 +161,18 @@
     def _():
         right[...] = jnp.zeros_like(right)
 
-    for copy in loads_out + loads_band + [load_in, load_kick]:
-        copy.wait()
-    row = lax.broadcasted_iota(jnp.int32, (ROW_BLOCK, ROW_BLOCK), 0)
-    col = lax.broadcasted_iota(jnp.int32, (ROW_BLOCK, ROW_BLOCK), 1)
-    for n in range(blocks):
-        head = band[n, :, :ROW_BLOCK].astype(jnp.float32)
-        band[n, :, :ROW_BLOCK] = jnp.where(col >= row, head, 0.0).astype(jnp.bfloat16)
-        tail = band[n, :, span - ROW_BLOCK :].astype(jnp.float32)
-        band[n, :, span - ROW_BLOCK :] = jnp.where(col <= row, tail, 0.0).astype(jnp.bfloat16)
-
-    neighbours = bits + jnp.where(has_left, 1, 0) + jnp.where(has_right, 1, 0)
+    def mask_band():
+        row = lax.broadcasted_iota(jnp.int32, (ROW_BLOCK, ROW_BLOCK), 0)
+        col = lax.broadcasted_iota(jnp.int32, (ROW_BLOCK, ROW_BLOCK), 1)
+        for n in range(blocks):
+            head = band[n, :, :ROW_BLOCK].astype(jnp.float32)
+            band[n, :, :ROW_BLOCK] = jnp.where(col >= row, head, 0.0).astype(jnp.bfloat16)
+            tail = band[n, :, span - ROW_BLOCK :].astype(jnp.float32)
+            band[n, :, span - ROW_BLOCK :] = jnp.where(col <= row, tail, 0.0).astype(
+                jnp.bfloat16
+            )
+
+    neighbours = len(offsets) + jnp.where(has_left, 1, 0) + jnp.where(has_right, 1, 0)
     pl.semaphore_wait(barrier, neighbours)
 
     def send_left(slot):
@@ -143,15 +195,34 @@
             device_id_type=MESH,
         )
 
-    def block_copy(slot, turn, m):
+    def block_copy(slot, rnd, q):
         return pltpu.make_async_remote_copy(
-            src_ref=snd.at[turn, m],
-            dst_ref=rbuf.at[slot, turn, m],
-            send_sem=blk_send.at[turn, m],
-            recv_sem=blk_recv.at[slot, turn, m],
-            device_id={"tile": partner((turn + m) % bits)},
+            src_ref=snd.at[rnd, q],
+            dst_ref=rbuf.at[slot, rnd, q],
+            send_sem=blk_send.at[rnd, q],
+            recv_sem=blk_recv.at[slot, rnd, q],
+            device_id={"tile": partner(offsets[q // cap])},
             device_id_type=MESH,
         )
+
+    def send_blocks(slot, rnd):
+        for q in range(slots):
+            chosen = blk[rnd, match - 1]
+            for m in range(match - 1):
+                chosen = jnp.where(route[rnd][m] == q, blk[rnd, m], chosen)
+            snd[rnd, q] = chosen
+            block_copy(slot, rnd, q).start()
+
+    def take_blocks(slot, rnd):
+        for q in range(slots):
+            block_copy(slot, rnd, q).wait_recv()
+        taken = [blk[rnd, m] for m in range(match)]
+        for q in range(slots):
+            came = rbuf[slot, rnd, q]
+            taken = [
+                jnp.where(route[rnd][m] == q, came, taken[m]) for m in range(match)
+            ]
+        return taken
 
     def own_band(n):
         start = hw - n * ROW_BLOCK
@@ -181,38 +252,44 @@
         def _():
             send_right(slot).start()
 
+        @pl.when(at == 0)
+        def _():
+            for copy in loads_out:
+                copy.wait()
+
         for m in range(match):
-            snd[0, m] = jnp.dot(
+            blk[0, m] = jnp.dot(
                 vb[...], tout[m], preferred_element_type=jnp.float32
             ).astype(jnp.bfloat16)
-            block_copy(slot, 0, m).start()
-        arrived = [None] * match
-        for turn in range(bits):
-            if turn == 0:
-                for n in range(blocks):
-                    own_band(n)
-            if turn == 1:
-
-                @pl.when(has_left)
-                def _():
-                    send_right(slot).wait_recv()
-
-                @pl.when(has_right)
-                def _():
-                    send_left(slot).wait_recv()
-
-                for n in range(blocks):
-                    halo_band(n, slot)
-            for m in range(match):
-                block_copy(slot, turn, m).wait_recv()
-                bit = (turn + m) % bits
-                chosen = ((masks_ref[m] // (1 << bit)) % 2) == 1
-                kept = jnp.where(chosen, rbuf[slot, turn, m], snd[turn, m])
-                if turn < bits - 1:
-                    snd[turn + 1, m] = kept
-                    block_copy(slot, turn + 1, m).start()
-                else:
-                    arrived[m] = kept * gate_ref[0, m].astype(jnp.float32).astype(jnp.bfloat16)
+        send_blocks(slot, 0)
+
+        @pl.when(at == 0)
+        def _():
+            for copy in loads_band + [load_in, load_kick]:
+                copy.wait()
+            mask_band()
+
+        for n in range(blocks):
+            own_band(n)
+        taken = take_blocks(slot, 0)
+        for m in range(match):
+            blk[1, m] = taken[m]
+        send_blocks(slot, 1)
+
+        @pl.when(has_left)
+        def _():
+            send_right(slot).wait_recv()
+
+        @pl.when(has_right)
+        def _():
+            send_left(slot).wait_recv()
+
+        for n in range(blocks):
+            halo_band(n, slot)
+        arrived = [
+            jnp.where(gates[m], block, jnp.zeros_like(block))
+            for m, block in enumerate(take_blocks(slot, 1))
+        ]
         tract = contract_last(arrived[0], tin[0])
         for m in range(1, match):
             tract = tract + contract_last(arrived[m], tin[m])
@@ -234,9 +311,9 @@
         def _():
             send_right(slot).wait_send()
 
-        for turn in range(bits):
-            for m in range(match):
-                block_copy(slot, turn, m).wait_send()
+        for rnd in range(2):
+            for q in range(slots):
+                block_copy(slot, rnd, q).wait_send()
         return carry
 
     lax.fori_loop(0, steps, step, 0)
@@ -255,6 +332,9 @@
 ):
     tile_count = lax.axis_size("tile")
     bits = tile_count.bit_length() - 1
+    low_bits = bits // 2 + bits % 2
+    low_count = 1 << low_bits
+    high_count = 1 << (bits - low_bits)
     rows, cols = voltage.shape
     steps = increments.shape[0]
     match, _, rank = tract_in.shape
@@ -265,32 +345,53 @@
     smem = pl.BlockSpec(memory_space=pltpu.SMEM)
     hbm = pl.BlockSpec(memory_space=pl.ANY)
     shape = jax.ShapeDtypeStruct((rows, cols), jnp.float32)
-    return pl.pallas_call(
-        functools.partial(field_kernel, tile_count),
-        out_shape=(shape, shape),
-        in_specs=[smem, smem, vmem, vmem, vmem, hbm, hbm, hbm, hbm],
-        out_specs=(vmem, vmem),
-        scratch_shapes=[
-            pltpu.VMEM((blocks, ROW_BLOCK, span), jnp.bfloat16),
-            pltpu.VMEM((match, cols, rank), jnp.bfloat16),
-            pltpu.VMEM((match, cols, rank), jnp.bfloat16),
-            pltpu.VMEM((steps, rows, cols), jnp.float32),
-            pltpu.VMEM((rows, cols), jnp.bfloat16),
-            pltpu.VMEM((2, rows, hw), jnp.bfloat16),
-            pltpu.VMEM((2, rows, hw), jnp.bfloat16),
-            pltpu.VMEM((rows, cols), jnp.float32),
-            pltpu.VMEM((bits, match, rows, rank), jnp.bfloat16),
-            pltpu.VMEM((2, bits, match, rows, rank), jnp.bfloat16),
-            pltpu.SemaphoreType.DMA((match + blocks + 2,)),
-            pltpu.SemaphoreType.DMA((2,)),
-            pltpu.SemaphoreType.DMA((2, 2)),
-            pltpu.SemaphoreType.DMA((bits, match)),
-            pltpu.SemaphoreType.DMA((2, bits, match)),
-        ],
-        compiler_params=pltpu.CompilerParams(
-            collective_id=0, has_side_effects=True, vmem_limit_bytes=50 * 1024 * 1024
-        ),
-    )(
+
+    def run(cap, *operands):
+        slots = cap * (low_count + high_count - 2)
+        return pl.pallas_call(
+            functools.partial(field_kernel, tile_count, cap),
+            out_shape=(shape, shape),
+            in_specs=[smem, smem, vmem, vmem, vmem, hbm, hbm, hbm, hbm],
+            out_specs=(vmem, vmem),
+            scratch_shapes=[
+                pltpu.VMEM((blocks, ROW_BLOCK, span), jnp.bfloat16),
+                pltpu.VMEM((match, cols, rank), jnp.bfloat16),
+                pltpu.VMEM((match, cols, rank), jnp.bfloat16),
+                pltpu.VMEM((steps, rows, cols), jnp.float32),
+                pltpu.VMEM((rows, cols), jnp.bfloat16),
+                pltpu.VMEM((2, rows, hw), jnp.bfloat16),
+                pltpu.VMEM((2, rows, hw), jnp.bfloat16),
+                pltpu.VMEM((rows, cols), jnp.float32),
+                pltpu.VMEM((2, match, rows, rank), jnp.bfloat16),
+                pltpu.VMEM((2, slots, rows, rank), jnp.bfloat16),
+                pltpu.VMEM((2, 2, slots, rows, rank), jnp.bfloat16),
+                pltpu.SemaphoreType.DMA((match + blocks + 2,)),
+                pltpu.SemaphoreType.DMA((2,)),
+                pltpu.SemaphoreType.DMA((2, 2)),
+                pltpu.SemaphoreType.DMA((2, slots)),
+                pltpu.SemaphoreType.DMA((2, 2, slots)),
+            ],
+            compiler_params=pltpu.CompilerParams(
+                collective_id=cap, has_side_effects=True, vmem_limit_bytes=50 * 1024 * 1024
+            ),
+        )(*operands)
+
+    masks = [matching_masks[m] for m in range(match)]
+    crowded = jnp.zeros((), jnp.bool_)
+    for one in range(match):
+        for two in range(one):
+            for three in range(two):
+                for part in (lambda k: k & (low_count - 1), lambda k: k >> low_bits):
+                    first = part(masks[one])
+                    crowded = crowded | (
+                        (first != 0)
+                        & (first == part(masks[two]))
+                        & (first == part(masks[three]))
+                    )
+    return lax.cond(
+        crowded,
+        functools.partial(run, (match + 1) // 2),
+        functools.partial(run, 1),
         matching_masks,
         tract_on,
         voltage,

time: 179 us -> 114 us (0.64)
  Pallas kernels: 170 us -> 105 us
  local copies, waits for them, and re-layouts: 8.02 us -> 2.72 us
  between operations: 0.66 us -> 5.64 us
    pallas_call x1, Pallas kernels: 170 us -> 105 us  [run(): pl.pallas_call(functools.partial(field_kernel, tile_count, cap), out_shap...]
    unnamed x16 -> x2, local copies, waits for them, and re-layouts: 8.02 us -> 1.31 us
where the time goes in v2:
time: 114 us; the launch traced here: 113 us
  Pallas kernels  105 us (92%)
  between operations  5.64 us (5%)
  local copies, waits for them, and re-layouts  2.72 us (2%)
    pallas_call x1, Pallas kernels, run(): pl.pallas_call(functools.partial(field_kernel, tile_count, cap), out_shap...  105 us

profile of v2, /device:TPU:0, one launch (start us, length us, event | category | flops | bytes accessed | tf_op | source)
XLA Modules:
  0.0 113.4 jit_solution(9360995932409455531)
XLA Ops:
  0.6 1.4 %fusion = (s32[1]{0:T(128)}, s32[1]{0:T(128)}, s32[1]{0:T(128)}, s32[1]{0:T(128)}) fusion(s32[4]{0:T(128)} %param.18), kind=kLoop, calls=%fused_computation | loop fusion | bytes 32 | tf_op jit(solution)/shard_map/slice | solution.py:379
  7.0 105.1 %conditional.1 = ((f32[32,1024]{1,0:T(8,128)S(1)}, f32[32,1024]{1,0:T(8,128)S(1)})) conditional(s32[]{:T(128)} %convert_element_type.3, (s32[4]{0:T(128)}, s32[1,4]{1,0:T(1,128)}, f32[32,1024]{1,0:T(8,128)}, f32[32,1024]{1,0:T(8,128)}, f32[1,1024]{1,0:T(1,128)}, /*index=5*/f32[10,32,1024]{2,1,0:T(8,128)}, bf16[1024,3072]{1,0:T(8,128)(2,1)}, ...), branch_computations={%region_0.0_spmd, %region_1.0_spmd} | conditional | bytes 8 | solution.py:391
  7.0 105.0 %branch_0_fun.1 = (f32[32,1024]{1,0:T(8,128)S(1)}, f32[32,1024]{1,0:T(8,128)S(1)}) custom-call(s32[4]{0:T(128)} %get-tuple-element.36.masks_ref, s32[1,4]{1,0:T(1,128)} %get-tuple-element.37.gate_ref, f32[32,1024]{1,0:T(8,128)} %get-tuple-element.38.v_in, f32[32,1024]{1,0:T(8,128)} %get-tuple-element.39.w_in, f32[1,1024]{1,0:T(1,128)} %get-tuple-element.40.scale_in, ...), custom_call_target="tpu_custom_call" | custom-call | tf_op jit(solution)/shard_map/cond/branch_0_fun/pallas_call | solution.py:351
  112.1 0.7 copy.21
  112.8 0.7 copy.22
